TPU v7x, 32 devices: a whole 2x2x4 slice. The times are simulated.
32 devices in a mesh: group: 2 (over y), expert: 8 (over z, core), tensor: 2 (over x).
Axes of the slice: x: 2, y: 2, z: 4, core: 2. Of those that a mesh axis runs over, the one named last changes fastest.
Arguments:
- tokens: bfloat16 [2048, 4096], P(('group', 'expert'), 'tensor'), parts along dimension 0, may hold values from -6 to 6
- expert_ids: int32 [2048, 4], P(('group', 'expert')), parts along dimension 0, may hold values from 0 to 7, all different within a row; in each aligned block of 128 rows (0 to 127, 128 to 255, ...) at most 96 rows name the same one
- gates: float32 [2048, 4], P(('group', 'expert')), parts along dimension 0, may hold values from 0.1 to 1
- gate_w: bfloat16 [8, 4096, 1536], P('expert', None, 'tensor'), may hold values from -0.09375 to 0.09375
- up_w: bfloat16 [8, 4096, 1536], P('expert', None, 'tensor'), may hold values from -0.09375 to 0.09375
- down_w: bfloat16 [8, 1536, 4096], P('expert', None, 'tensor'), may hold values from -0.15625 to 0.15625
Outputs:
- mixed: bfloat16 [2048, 4096], P(('group', 'expert'), 'tensor'), parts along dimension 0
There are 2 independent parts, one for each index of `group`. A program takes and returns all parts, laid end to end along the dimension named above; an argument that names none is the same for every part. Nothing has to cross between parts.
Inputs may be any that keep to these rules, and one draw needn't show every extreme that they name: `expert_ids`: A row names 4 different experts. Among the rows of one index of the expert axis no expert is named by more than 96 rows, a bound that some block reaches of them.
All inputs are finite; a program needn't handle non-finite values.
Results may differ from a plain program's by a relative error of at most 0.0057.
Values may be sent and summed in bfloat16 or wider, within the bound.
A program may use at most 128 MiB of HBM per device.

v0:
```python
import jax
import jax.numpy as jnp
from jax import lax
from jax.sharding import PartitionSpec as P


def on_device(tokens, expert_ids, gates, gate_w, up_w, down_w):
    peers = lax.axis_size("expert")
    rows, top = expert_ids.shape
    capacity = min(rows, 3 * rows * top // (2 * peers))
    total_slots = peers * capacity
    flat_ids = expert_ids.reshape(rows * top)
    onehot = (flat_ids[:, None] == jnp.arange(peers, dtype=jnp.int32)[None, :]).astype(jnp.int32)
    earlier = jnp.cumsum(onehot, 0) - onehot
    rank = jnp.sum(earlier * onehot, 1)
    counts = jnp.sum(onehot, 0).reshape(peers, 1)
    slot = flat_ids * capacity + rank
    source_row = jnp.arange(rows * top, dtype=jnp.int32) // top
    whole = lax.all_gather(tokens, "tensor", axis=1, tiled=True)
    buffer = jnp.zeros((total_slots, whole.shape[1]), whole.dtype)
    buffer = buffer.at[slot].set(whole[source_row])
    arrived = lax.all_to_all(
        buffer.reshape(peers, capacity, whole.shape[1]),
        "expert",
        split_axis=0,
        concat_axis=0,
        tiled=True,
    )
    arrived_counts = lax.all_to_all(counts, "expert", split_axis=0, concat_axis=0, tiled=True)
    slots_in = arrived.reshape(total_slots, arrived.shape[2])
    got = arrived_counts.reshape(peers)
    offsets = jnp.cumsum(got) - got
    live = jnp.sum(got)
    local_slot = jnp.arange(capacity, dtype=jnp.int32)
    valid = local_slot[None, :] < got[:, None]
    packed_pos = jnp.where(valid, offsets[:, None] + local_slot[None, :], total_slots).reshape(
        total_slots
    )
    order = (
        jnp.zeros((total_slots + 1,), jnp.int32)
        .at[packed_pos]
        .set(jnp.arange(total_slots, dtype=jnp.int32))
    )
    order = order[:total_slots]
    block = min(128, total_slots)
    steps = (live + block - 1) // block
    weight_gate = gate_w[0]
    weight_up = up_w[0]
    weight_down = down_w[0]
    hidden_share = weight_gate.shape[1]
    feat_share = weight_down.shape[1]

    def hidden_block(index):
        picks = lax.dynamic_slice_in_dim(order, index * block, block)
        picked = slots_in[picks]
        gate_part = jnp.dot(picked, weight_gate, preferred_element_type=jnp.float32)
        up_part = jnp.dot(picked, weight_up, preferred_element_type=jnp.float32)
        hidden = (jax.nn.silu(gate_part) * up_part).astype(jnp.bfloat16)
        inside = index * block + jnp.arange(block, dtype=jnp.int32) < live
        target = jnp.where(inside, picks, total_slots)
        return (target, hidden)

    def store_hidden(index, store):
        target, hidden = hidden_block(index)
        return store.at[target].set(hidden)

    store = lax.fori_loop(
        0, steps, store_hidden, jnp.zeros((total_slots + 1, hidden_share), jnp.bfloat16)
    )
    hidden_all = store[:total_slots]
    result = jnp.dot(
        lax.all_gather(hidden_all, "tensor", axis=1, tiled=True),
        weight_down,
        preferred_element_type=jnp.float32,
    ).astype(jnp.bfloat16)
    returned = lax.all_to_all(
        result.reshape(peers, capacity, feat_share),
        "expert",
        split_axis=0,
        concat_axis=0,
        tiled=True,
    )
    mine = returned.reshape(total_slots, feat_share)[slot].reshape(rows, top, feat_share)
    combined = jnp.sum(gates[:, :, None] * mine.astype(jnp.float32), 1)
    return combined.astype(jnp.bfloat16)


def solution(mesh):
    in_specs = (
        P(("group", "expert"), "tensor"),
        P(("group", "expert"), None),
        P(("group", "expert"), None),
        P("expert", None, "tensor"),
        P("expert", None, "tensor"),
        P("expert", None, "tensor"),
    )
    out_specs = P(("group", "expert"), "tensor")
    return jax.shard_map(
        on_device, mesh=mesh, in_specs=in_specs, out_specs=out_specs, check_vma=False
    )
```

profile of v0, /device:TPU:0, one launch (start us, length us, event | category | flops | bytes accessed | tf_op | source)
XLA Modules:
  0.0 422.7 jit_solution(6958448967155949487)
XLA Ops:
  6.5 0.7 all-gather.3.cloned.1.call-update
  7.3 0.8 copy.18
  8.2 0.1 eq.25
  8.3 1.1 reduce-window.19
  9.4 0.2 slice_reduce_fusion
  9.7 0.1 fusion.10
  9.8 0.7 copy.19
  10.5 6.3 %all-to-all-start = ((s32[8,1,1]{2,1,0:T(1,128)}), s32[8,1,1]{2,1,0:T(1,128)S(1)}, u32[]{:S(2)}, u32[]{:S(2)}) async-start(s32[8,1,1]{2,1,0:T(1,128)} %copy.19), calls=%async_computation | async-start | bytes 8192 | tf_op jit(solution)/shard_map/all_to_all | solution.py:29
  16.8 0.7 broadcast_multiply_fusion
  17.5 0.1 copy.20
  17.6 0.1 mul.41
  17.8 15.2 %all-gather.3.cloned.1.call-done = bf16[128,4096]{1,0:T(8,128)(2,1)} async-done(((bf16[128,2048]{1,0:T(8,128)(2,1)}), bf16[128,4096]{1,0:T(8,128)(2,1)}) %all-gather.3.cloned.1.call-update) | async-done | bytes 1048592 | tf_op jit(solution)/shard_map/all_gather | solution.py:19
  32.9 20.2 %scatter_custom_fusion.2 = bf16[768,4096]{1,0:T(8,128)(2,1)} fusion(s32[512]{0:T(512)S(1)} %bitcast.42, bf16[128,4096]{1,0:T(8,128)(2,1)} %all-gather.3.cloned.1.call-done, s32[1024]{0:T(1024)S(1)} %pad_clamp_fusion.2, bf16[]{:T(256)} %constant.62.clone.1), kind=kCustom, calls=%fused_computation.14 | custom fusion | bytes 6291968 | tf_op jit(solution)/shard_map/scatter | solution.py:21
  53.1 4.7 %all-to-all-start.1 = ((bf16[8,96,4096]{2,1,0:T(8,128)(2,1)}), bf16[8,96,4096]{2,1,0:T(8,128)(2,1)}, u32[]{:S(2)}, u32[]{:S(2)}) async-start(bf16[8,96,4096]{2,1,0:T(8,128)(2,1)} %bitcast.39), calls=%async_computation.1 | async-start | bytes 12582912 | tf_op jit(solution)/shard_map/all_to_all | solution.py:22
  57.9 0.8 fusion.15
  59.3 0.2 reduce-window.18
  59.7 3.4 scatter_custom_fusion.1
  63.1 133.7 %all-to-all-done.1 = bf16[8,96,4096]{2,1,0:T(8,128)(2,1)} async-done(((bf16[8,96,4096]{2,1,0:T(8,128)(2,1)}), bf16[8,96,4096]{2,1,0:T(8,128)(2,1)}, u32[]{:S(2)}, u32[]{:S(2)}) %all-to-all-start.1) | async-done | bytes 6291488 | tf_op jit(solution)/shard_map/all_to_all | solution.py:22
  196.9 84.1 %while.10 = (s32[]{:T(128)}, bf16[769,768]{1,0:T(8,128)(2,1)S(1)}, s32[]{:T(128)}, s32[]{:T(128)}, s32[768]{0:T(1024)S(1)}, /*index=5*/bf16[768,4096]{1,0:T(8,12...) while((s32[]{:T(128)}, bf16[769,768]{1,0:T(8,128)(2,1)S(1)}, ...), condition=%wide.region_10.11_spmd, body=%wide.region_8.10_spmd.sunk | while | flops 1611204736 | bytes 43523272 | solution.py:67
  196.9 0.7 compare_select_fusion.7
  197.6 5.8 %gather_fusion = bf16[128,4096]{1,0:T(8,128)(2,1)S(1)} fusion(bf16[768,4096]{1,0:T(8,128)(2,1)} %get-tuple-element.154, s32[1024]{0:T(1024)S(1)} %pad_clamp_fusion.4), kind=kCustom, calls=%fused_computation.clone.1 | custom fusion | bytes 2097664 | tf_op jit(solution)/shard_map/while/body/gather | solution.py:55
  203.4 3.9 fusion.32
  207.4 0.6 copy-done
  208.0 1.1 fusion.33
  209.1 1.8 scatter_fusion
  210.9 0.7 compare_select_fusion.7
  211.6 5.8 %gather_fusion = bf16[128,4096]{1,0:T(8,128)(2,1)S(1)} fusion(bf16[768,4096]{1,0:T(8,128)(2,1)} %get-tuple-element.154, s32[1024]{0:T(1024)S(1)} %pad_clamp_fusion.4), kind=kCustom, calls=%fused_computation.clone.1 | custom fusion | bytes 2097664 | tf_op jit(solution)/shard_map/while/body/gather | solution.py:55
  217.4 3.9 fusion.32
  221.3 0.6 copy-done
  222.0 1.1 fusion.33
  223.1 1.8 scatter_fusion
  224.9 0.7 compare_select_fusion.7
  225.6 5.8 %gather_fusion = bf16[128,4096]{1,0:T(8,128)(2,1)S(1)} fusion(bf16[768,4096]{1,0:T(8,128)(2,1)} %get-tuple-element.154, s32[1024]{0:T(1024)S(1)} %pad_clamp_fusion.4), kind=kCustom, calls=%fused_computation.clone.1 | custom fusion | bytes 2097664 | tf_op jit(solution)/shard_map/while/body/gather | solution.py:55
  231.4 3.9 fusion.32
  235.3 0.6 copy-done
  236.0 1.1 fusion.33
  237.1 1.8 scatter_fusion
  238.8 0.7 compare_select_fusion.7
  239.5 5.8 %gather_fusion = bf16[128,4096]{1,0:T(8,128)(2,1)S(1)} fusion(bf16[768,4096]{1,0:T(8,128)(2,1)} %get-tuple-element.154, s32[1024]{0:T(1024)S(1)} %pad_clamp_fusion.4), kind=kCustom, calls=%fused_computation.clone.1 | custom fusion | bytes 2097664 | tf_op jit(solution)/shard_map/while/body/gather | solution.py:55
  245.4 3.9 fusion.32
  249.3 0.6 copy-done
  249.9 1.1 fusion.33
  251.0 1.8 scatter_fusion
  252.8 0.7 compare_select_fusion.7
  253.5 5.8 %gather_fusion = bf16[128,4096]{1,0:T(8,128)(2,1)S(1)} fusion(bf16[768,4096]{1,0:T(8,128)(2,1)} %get-tuple-element.154, s32[1024]{0:T(1024)S(1)} %pad_clamp_fusion.4), kind=kCustom, calls=%fused_computation.clone.1 | custom fusion | bytes 2097664 | tf_op jit(solution)/shard_map/while/body/gather | solution.py:55
  259.3 3.9 fusion.32
  263.3 0.6 copy-done
  263.9 1.1 fusion.33
  265.0 1.8 scatter_fusion
  266.8 0.7 compare_select_fusion.7
  267.5 5.8 %gather_fusion = bf16[128,4096]{1,0:T(8,128)(2,1)S(1)} fusion(bf16[768,4096]{1,0:T(8,128)(2,1)} %get-tuple-element.154, s32[1024]{0:T(1024)S(1)} %pad_clamp_fusion.4), kind=kCustom, calls=%fused_computation.clone.1 | custom fusion | bytes 2097664 | tf_op jit(solution)/shard_map/while/body/gather | solution.py:55
  273.3 3.9 fusion.32
  277.3 0.6 copy-done
  277.9 1.1 fusion.33
  279.0 1.8 scatter_fusion
  281.0 1.1 slice.15
  282.1 34.1 %all-gather.5.cloned.1.call-done = bf16[768,1536]{1,0:T(8,128)(2,1)} async-done(((bf16[768,768]{1,0:T(8,128)(2,1)}), bf16[768,1536]{1,0:T(8,128)(2,1)}) %all-gather.5.cloned.1.call-update) | async-done | bytes 2359312 | tf_op jit(solution)/shard_map/all_gather | solution.py:72
  316.3 9.0 %fusion.5 = bf16[768,2048]{1,0:T(8,128)(2,1)} fusion(bf16[768,1536]{1,0:T(8,128)(2,1)} %all-gather.5.cloned.1.call-done, bf16[1,1536,2048]{2,1,0:T(8,128)(2,1)} %param.13), kind=kOutput, calls=%fused_computation.17 | convolution fusion | flops 4833411072 | bytes 11796480 | tf_op jit(solution)/shard_map/dot_general | solution.py:71
  325.3 4.7 %all-to-all-start.2 = ((bf16[8,96,2048]{2,1,0:T(8,128)(2,1)}), bf16[8,96,2048]{2,1,0:T(8,128)(2,1)S(1)}, u32[]{:S(2)}, u32[]{:S(2)}) async-start(bf16[8,96,2048]{2,1,0:T(8,128)(2,1)} %bitcast.40), calls=%async_computation.2 | async-start | bytes 6291456 | tf_op jit(solution)/shard_map/all_to_all | solution.py:76
  330.0 0.1 copy.17
  330.2 71.4 %all-to-all-done.2 = bf16[8,96,2048]{2,1,0:T(8,128)(2,1)S(1)} async-done(((bf16[8,96,2048]{2,1,0:T(8,128)(2,1)}), bf16[8,96,2048]{2,1,0:T(8,128)(2,1)S(1)}, u32[]{:S(2)}, u32[]{:S(2)}) %all-to-all-start.2) | async-done | bytes 3145760 | tf_op jit(solution)/shard_map/all_to_all | solution.py:76
  401.6 3.3 gather_fusion.1
  404.9 4.8 %reshape.201 = f32[128,4,2048]{2,1,0:T(4,128)} reshape(bf16[512,2048]{1,0:T(8,128)(2,1)} %gather_fusion.1) | data formatting | bytes 6291456 | tf_op jit(solution)/shard_map/convert_element_type | solution.py:84
  409.6 6.2 %multiply_reduce_fusion = bf16[128,2048]{1,0:T(8,128)(2,1)} fusion(f32[128,4,2048]{2,1,0:T(4,128)} %reshape.201, f32[128,4]{1,0:T(8,128)S(1)} %copy.17), kind=kLoop, calls=%fused_computation.16 | loop fusion | flops 1835008 | bytes 4720640 | tf_op jit(solution)/shard_map/reduce_sum | solution.py:84
  (32 shorter events, 0.6 us)
Async XLA Ops:
  6.5 26.4 %all-gather.3.cloned.1.call-start = ((), (), s32[]{:S(2)}) async-start(), calls=%async_computation.3 | async-start | bytes 1572864 | tf_op jit(solution)/shard_map/all_gather | solution.py:19
  10.5 42.6 %all-to-all-start = ((s32[8,1,1]{2,1,0:T(1,128)}), s32[8,1,1]{2,1,0:T(1,128)S(1)}, u32[]{:S(2)}, u32[]{:S(2)}) async-start(s32[8,1,1]{2,1,0:T(1,128)} %copy.19), calls=%async_computation | async-start | bytes 8192 | tf_op jit(solution)/shard_map/all_to_all | solution.py:29
  53.1 143.7 %all-to-all-start.1 = ((bf16[8,96,4096]{2,1,0:T(8,128)(2,1)}), bf16[8,96,4096]{2,1,0:T(8,128)(2,1)}, u32[]{:S(2)}, u32[]{:S(2)}) async-start(bf16[8,96,4096]{2,1,0:T(8,128)(2,1)} %bitcast.39), calls=%async_computation.1 | async-start | bytes 12582912 | tf_op jit(solution)/shard_map/all_to_all | solution.py:22
  57.8 258.4 %all-gather.5.cloned.1.call-start = ((), (), s32[]{:S(2)}) async-start(), calls=%async_computation.4 | async-start | bytes 3538944 | tf_op jit(solution)/shard_map/all_gather | solution.py:72
  203.4 4.6 %copy-start = (bf16[4096,768]{1,0:T(8,128)(2,1)S(1)}, bf16[4096,768]{1,0:T(8,128)(2,1)}, u32[]{:S(2)}) copy-start(bf16[4096,768]{1,0:T(8,128)(2,1)} %get-tuple-element.156) | copy-start | bytes 18874372 | tf_op jit(solution)/shard_map/while
  217.4 4.6 %copy-start = (bf16[4096,768]{1,0:T(8,128)(2,1)S(1)}, bf16[4096,768]{1,0:T(8,128)(2,1)}, u32[]{:S(2)}) copy-start(bf16[4096,768]{1,0:T(8,128)(2,1)} %get-tuple-element.156) | copy-start | bytes 18874372 | tf_op jit(solution)/shard_map/while
  231.4 4.6 %copy-start = (bf16[4096,768]{1,0:T(8,128)(2,1)S(1)}, bf16[4096,768]{1,0:T(8,128)(2,1)}, u32[]{:S(2)}) copy-start(bf16[4096,768]{1,0:T(8,128)(2,1)} %get-tuple-element.156) | copy-start | bytes 18874372 | tf_op jit(solution)/shard_map/while
  245.3 4.6 %copy-start = (bf16[4096,768]{1,0:T(8,128)(2,1)S(1)}, bf16[4096,768]{1,0:T(8,128)(2,1)}, u32[]{:S(2)}) copy-start(bf16[4096,768]{1,0:T(8,128)(2,1)} %get-tuple-element.156) | copy-start | bytes 18874372 | tf_op jit(solution)/shard_map/while
  259.3 4.6 %copy-start = (bf16[4096,768]{1,0:T(8,128)(2,1)S(1)}, bf16[4096,768]{1,0:T(8,128)(2,1)}, u32[]{:S(2)}) copy-start(bf16[4096,768]{1,0:T(8,128)(2,1)} %get-tuple-element.156) | copy-start | bytes 18874372 | tf_op jit(solution)/shard_map/while
  273.3 4.6 %copy-start = (bf16[4096,768]{1,0:T(8,128)(2,1)S(1)}, bf16[4096,768]{1,0:T(8,128)(2,1)}, u32[]{:S(2)}) copy-start(bf16[4096,768]{1,0:T(8,128)(2,1)} %get-tuple-element.156) | copy-start | bytes 18874372 | tf_op jit(solution)/shard_map/while
  325.3 4.7 %copy-start.1 = (f32[128,4]{0,1:T(4,128)S(1)}, f32[128,4]{0,1:T(4,128)}, u32[]{:S(2)}) copy-start(f32[128,4]{0,1:T(4,128)} %param.10) | copy-start | bytes 6148
  325.3 76.3 %all-to-all-start.2 = ((bf16[8,96,2048]{2,1,0:T(8,128)(2,1)}), bf16[8,96,2048]{2,1,0:T(8,128)(2,1)S(1)}, u32[]{:S(2)}, u32[]{:S(2)}) async-start(bf16[8,96,2048]{2,1,0:T(8,128)(2,1)} %bitcast.40), calls=%async_computation.2 | async-start | bytes 6291456 | tf_op jit(solution)/shard_map/all_to_all | solution.py:76
Sparse Core Ops, SparseCore 0:
  8.9 23.9 all-gather.2
  282.2 33.9 all-gather.4
where the time goes:
time: 423 us
  waiting for transfers between devices  255 us (60%)
  local copies, waits for them, and re-layouts  84.4 us (20%)
  matrix products  39.1 us (9%)
  starting transfers between devices  15.8 us (4%)
  between operations  14.1 us (3%)
  other arithmetic  13.5 us (3%)
    all_to_all x1, waiting for transfers between devices, on_device(): lax.all_to_all(buffer.reshape(peers, capacity, whole.shape[1]), 'expert',...  134 us
    all_to_all x1, waiting for transfers between devices, on_device(): lax.all_to_all(result.reshape(peers, capacity, feat_share), 'expert', spl...  71.4 us
    gather x6, local copies, waits for them, and re-layouts, hidden_block(): picked = slots_in[picks]  34.8 us
    all_gather x1, waiting for transfers between devices, on_device(): lax.all_gather(hidden_all, 'tensor', axis=1, tiled=True)  34.1 us
    dot_general x6, matrix products, hidden_block(): gate_part = jnp.dot(picked, weight_gate, preferred_element_type=jnp.float32)  23.6 us
    scatter x1, local copies, waits for them, and re-layouts, on_device(): buffer = buffer.at[slot].set(whole[source_row])  20.2 us
    all_gather x1, waiting for transfers between devices, on_device(): whole = lax.all_gather(tokens, 'tensor', axis=1, tiled=True)  15.2 us
    scatter x6, local copies, waits for them, and re-layouts, store_hidden(): return store.at[target].set(hidden)  10.6 us
  transfers between devices with their start and end apart: 5, of which 4 were waited for; matrix products, arithmetic and copies ran while one was open for 7% of the time, Pallas kernels for 0%

commit v1 on v0

v1 whole, which is shorter than its diff:
```python
import jax
import jax.numpy as jnp
from jax import lax
from jax.sharding import PartitionSpec as P


def on_device(tokens, expert_ids, gates, gate_w, up_w, down_w):
    me = lax.axis_index("expert")
    whole = lax.all_gather(tokens, "tensor", axis=1, tiled=True)
    rows_all = lax.all_gather(whole, "expert", axis=0, tiled=True)
    peers = lax.axis_size("expert")
    own = jnp.sum(
        jnp.where(
            expert_ids[:, :, None] == jnp.arange(peers, dtype=jnp.int32)[None, None, :],
            gates[:, :, None],
            0.0,
        ),
        1,
    )
    weight = lax.dynamic_slice_in_dim(lax.all_gather(own, "expert", axis=0, tiled=True), me, 1, 1)
    gate_part = jnp.dot(rows_all, gate_w[0], preferred_element_type=jnp.float32)
    up_part = jnp.dot(rows_all, up_w[0], preferred_element_type=jnp.float32)
    hidden = (jax.nn.silu(gate_part) * up_part).astype(jnp.bfloat16)
    hidden = lax.all_gather(hidden, "tensor", axis=1, tiled=True)
    result = jnp.dot(hidden, down_w[0], preferred_element_type=jnp.float32)
    share = (result * weight).astype(jnp.bfloat16)
    return lax.psum_scatter(share, "expert", scatter_dimension=0, tiled=True)


def solution(mesh):
    in_specs = (
        P(("group", "expert"), "tensor"),
        P(("group", "expert"), None),
        P(("group", "expert"), None),
        P("expert", None, "tensor"),
        P("expert", None, "tensor"),
        P("expert", None, "tensor"),
    )
    out_specs = P(("group", "expert"), "tensor")
    return jax.shard_map(
        on_device, mesh=mesh, in_specs=in_specs, out_specs=out_specs, check_vma=False
    )
```

time: 423 us -> 250 us (0.59)
  local copies, waits for them, and re-layouts: 84.4 us -> 0.02 us
  waiting for transfers between devices: 255 us -> 190 us
  starting transfers between devices: 15.8 us -> 0.12 us
  blocking collectives: 0 us -> 14 us
  other arithmetic: 13.5 us -> 0.01 us
  matrix products: 39.1 us -> 33 us
    all_to_all x3 -> x0, waiting for transfers between devices: 205 us -> none  [the longest x1 134 us: on_device(): lax.all_to_all(buffer.reshape(peers, capacity, whole.shape[1]), 'expert',...]
    all_gather x1 -> x2, waiting for transfers between devices: 34.1 us -> 113 us  [the longest x1 83.6 us: on_device(): rows_all = lax.all_gather(whole, 'expert', axis=0, tiled=True)]
    reduce_scatter x0 -> x1, waiting for transfers between devices: none -> 50.2 us  [on_device(): return lax.psum_scatter(share, 'expert', scatter_dimension=0, tiled=True)]
    gather x7 -> x0, local copies, waits for them, and re-layouts: 38.1 us -> none  [the longest x6 34.8 us: hidden_block(): picked = slots_in[picks]]
    scatter x8 -> x0, local copies, waits for them, and re-layouts: 34.1 us -> none  [the longest x1 20.2 us: on_device(): buffer = buffer.at[slot].set(whole[source_row])]
    all_to_all x3 -> x0, starting transfers between devices: 15.8 us -> none  [the longest x1 6.33 us: on_device(): lax.all_to_all(counts, 'expert', split_axis=0, concat_axis=0, tiled=True)]
    all_gather x0 -> x1, blocking collectives: none -> 14 us  [on_device(): lax.all_gather(own, 'expert', axis=0, tiled=True)]
    all_gather x1, waiting for transfers between devices: 15.2 us -> 25.6 us  [on_device(): whole = lax.all_gather(tokens, 'tensor', axis=1, tiled=True)]
  transfers between devices with their start and end apart: 5 -> 4, of which waited for: 4 -> 4; matrix products, arithmetic and copies ran while one was open for 7% -> 0% of each run, Pallas kernels for 0% -> 0%
where the time goes in v1:
time: 250 us
  waiting for transfers between devices  190 us (76%)
  matrix products  33 us (13%)
  blocking collectives  14 us (6%)
  between operations  13.2 us (5%)
    all_gather x1, waiting for transfers between devices, on_device(): rows_all = lax.all_gather(whole, 'expert', axis=0, tiled=True)  83.6 us
    reduce_scatter x1, waiting for transfers between devices, on_device(): return lax.psum_scatter(share, 'expert', scatter_dimension=0, tiled=True)  50.2 us
    all_gather x1, waiting for transfers between devices, on_device(): hidden = lax.all_gather(hidden, 'tensor', axis=1, tiled=True)  29.5 us
    all_gather x1, waiting for transfers between devices, on_device(): whole = lax.all_gather(tokens, 'tensor', axis=1, tiled=True)  25.6 us
    all_gather x1, blocking collectives, on_device(): lax.all_gather(own, 'expert', axis=0, tiled=True)  14 us
    dot_general x1, matrix products, on_device(): result = jnp.dot(hidden, down_w[0], preferred_element_type=jnp.float32)  11 us
    dot_general x1, matrix products, on_device(): up_part = jnp.dot(rows_all, up_w[0], preferred_element_type=jnp.float32)  11 us
    dot_general x1, matrix products, on_device(): gate_part = jnp.dot(rows_all, gate_w[0], preferred_element_type=jnp.float32)  11 us
  transfers between devices with their start and end apart: 4, of which 4 were waited for; matrix products, arithmetic and copies ran while one was open for 0% of the time, Pallas kernels for 0%

profile of v1, /device:TPU:0, one launch (start us, length us, event | category | flops | bytes accessed | tf_op | source)
XLA Modules:
  0.0 250.1 jit_solution(12539147457305482302)
XLA Ops:
  6.5 0.0 all-gather.4.cloned.1.call-start
  6.5 0.7 all-gather.4.cloned.1.call-update
  7.3 0.0 all-gather.6.cloned.1.call-start
  7.3 25.6 %all-gather.4.cloned.1.call-done = bf16[128,4096]{1,0:T(8,128)(2,1)} async-done(((bf16[128,2048]{1,0:T(8,128)(2,1)}), bf16[128,4096]{1,0:T(8,128)(2,1)}) %all-gather.4.cloned.1.call-update) | async-done | bytes 1048592 | tf_op jit(solution)/shard_map/all_gather | solution.py:9
  32.9 0.0 all-gather.6.cloned.1.call-update
  33.0 0.0 all-gather.8.cloned.1.call-start
  33.0 83.6 %all-gather.6.cloned.1.call-done = bf16[1024,4096]{1,0:T(8,128)(2,1)} async-done(((bf16[128,4096]{1,0:T(8,128)(2,1)}), bf16[1024,4096]{1,0:T(8,128)(2,1)}) %all-gather.6.cloned.1.call-update) | async-done | bytes 8388624 | tf_op jit(solution)/shard_map/all_gather | solution.py:10
  116.6 0.0 copy-start.2
  116.6 11.0 %fusion.2 = f32[1024,768]{1,0:T(8,128)S(1)} fusion(bf16[1024,4096]{1,0:T(8,128)(2,1)} %all-gather.6.cloned.1.call-done, bf16[1,4096,768]{2,1,0:T(8,128)(2,1)} %param.10), kind=kOutput, calls=%fused_computation.3 | convolution fusion | flops 6442450944 | bytes 17825792 | tf_op jit(solution)/shard_map/dot_general | solution.py:22
  127.7 0.0 copy-done.2
  127.7 0.0 copy-start
  127.7 0.0 copy-start.1
  127.7 11.0 %multiply_convert_fusion.1 = bf16[1024,768]{1,0:T(8,128)(2,1)} fusion(f32[1024,768]{1,0:T(8,128)S(1)} %fusion.2, bf16[1024,4096]{1,0:T(8,128)(2,1)S(1)} %copy-done.2, bf16[1,4096,768]{2,1,0:T(8,128)(2,1)} %param.9), kind=kOutput, calls=%fused_computation.7 | convolution fusion | flops 6447169536 | bytes 19398656 | tf_op jit(solution)/shard_map/dot_general | solution.py:21
  138.7 0.0 all-gather.8.cloned.1.call-update
  138.7 0.0 reduce-scatter.2.cloned.1.call-start
  138.8 0.0 copy-done
  138.8 0.0 copy-done.1
  138.8 14.0 %all_gather.15 = f32[1024,8]{0,1:T(8,128)S(1)} all-gather(f32[128,8]{0,1:T(8,128)S(1)} %select_reduce_fusion), channel_id=1, replica_groups=mesh['group'=2,'expert'=8,'tensor'=2] {'expert'}, dimensions={0}, use_global_device_ids=true | all-gather | bytes 36864 | tf_op jit(solution)/shard_map/all_gather | solution.py:20
  152.8 29.5 %all-gather.8.cloned.1.call-done = bf16[1024,1536]{1,0:T(8,128)(2,1)} async-done(((bf16[1024,768]{1,0:T(8,128)(2,1)}), bf16[1024,1536]{1,0:T(8,128)(2,1)}) %all-gather.8.cloned.1.call-update) | async-done | bytes 3145744 | tf_op jit(solution)/shard_map/all_gather | solution.py:24
  182.3 11.0 %multiply_convert_fusion = bf16[1024,2048]{1,0:T(8,128)(2,1)} fusion(f32[1024]{0:T(1024)S(1)} %bitcast.17, bf16[1024,1536]{1,0:T(8,128)(2,1)} %all-gather.8.cloned.1.call-done, bf16[1,1536,2048]{2,1,0:T(8,128)(2,1)} %param.11), kind=kOutput, calls=%fused_computation | convolution fusion | flops 6446645248 | bytes 13635584 | tf_op jit(solution)/shard_map/dot_general | solution.py:25
  193.4 0.0 reduce-scatter.2.cloned.1.call-update
  193.4 50.2 %reduce-scatter.2.cloned.1.call-done = bf16[128,2048]{1,0:T(8,128)(2,1)} async-done(((bf16[1024,2048]{1,0:T(8,128)(2,1)}), bf16[128,2048]{1,0:T(8,128)(2,1)}) %reduce-scatter.2.cloned.1.call-update) | async-done | bytes 524304 | tf_op jit(solution)/shard_map/reduce_scatter | solution.py:27
  (2 shorter events, 0.0 us)
Async XLA Ops:
  6.5 26.4 %all-gather.4.cloned.1.call-start = ((), (), s32[]{:S(2)}) async-start(), calls=%async_computation.1 | async-start | bytes 1572864 | tf_op jit(solution)/shard_map/all_gather | solution.py:9
  7.3 109.4 %all-gather.6.cloned.1.call-start = ((), (), s32[]{:S(2)}) async-start(), calls=%async_computation.2 | async-start | bytes 9437184 | tf_op jit(solution)/shard_map/all_gather | solution.py:10
  33.0 149.4 %all-gather.8.cloned.1.call-start = ((), (), s32[]{:S(2)}) async-start(), calls=%async_computation.3 | async-start | bytes 4718592 | tf_op jit(solution)/shard_map/all_gather | solution.py:24
  116.6 11.0 %copy-start.2 = (bf16[1024,4096]{1,0:T(8,128)(2,1)S(1)}, bf16[1024,4096]{1,0:T(8,128)(2,1)}, u32[]{:S(2)}) copy-start(bf16[1024,4096]{1,0:T(8,128)(2,1)} %all-gather.6.cloned.1.call-done) | copy-start | bytes 25165828
  127.7 11.1 %copy-start = (f32[128,4]{0,1:T(4,128)S(1)}, f32[128,4]{0,1:T(4,128)}, u32[]{:S(2)}) copy-start(f32[128,4]{0,1:T(4,128)} %param.8) | copy-start | bytes 6148
  127.7 11.1 %copy-start.1 = (s32[128,4]{0,1:T(4,128)S(1)}, s32[128,4]{0,1:T(4,128)}, u32[]{:S(2)}) copy-start(s32[128,4]{0,1:T(4,128)} %param.7) | copy-start | bytes 6148
  138.7 104.8 %reduce-scatter.2.cloned.1.call-start = ((), (), s32[]{:S(2)}) async-start(), calls=%async_computation.4 | async-start | bytes 4718592 | tf_op jit(solution)/shard_map/reduce_scatter | solution.py:27
Sparse Core Ops, SparseCore 0:
  8.9 23.9 all-gather.3
  34.5 82.0 all-gather.5
  138.8 43.4 all-gather.7
  193.5 50.0 reduce-scatter.1

commit v2 on v1

--- a/solution.py
+++ b/solution.py
@@ -1,10 +1,12 @@
 import jax
 import jax.numpy as jnp
 from jax import lax
+from jax.experimental import pallas as pl
+from jax.experimental.pallas import tpu as pltpu
 from jax.sharding import PartitionSpec as P
 
 
-def on_device(tokens, expert_ids, gates, gate_w, up_w, down_w):
+def dense(tokens, expert_ids, gates, gate_w, up_w, down_w):
     me = lax.axis_index("expert")
     whole = lax.all_gather(tokens, "tensor", axis=1, tiled=True)
     rows_all = lax.all_gather(whole, "expert", axis=0, tiled=True)
@@ -27,6 +29,306 @@
     return lax.psum_scatter(share, "expert", scatter_dimension=0, tiled=True)
 
 
+MESH = pl.DeviceIdType.MESH
+CHIPS = 4
+TILE = 256
+DOWN_TILE = 512
+
+
+def kernel(
+    tokens, own, gate_hbm, up_hbm, down_hbm, out,
+    x_all, gate_w, up_w, down_w, hid, res, to_sib, from_sib, to_chip, from_chip, acc, wt,
+    load_sem, z_send, x_send, s_send, w_send, h_send, r_send, c_send,
+    z_recv, x_recv, s_recv, w_recv, h_recv, r_recv, c_recv,
+):
+    e = lax.axis_index("expert")
+    x = lax.axis_index("tensor")
+    z, c = lax.div(e, 2), lax.rem(e, 2)
+    half = lax.div(z, 2)
+    other = 1 - x
+    x_peer = {"tensor": other}
+    sibling = {"expert": z * 2 + 1 - c}
+    rows = pl.ds(pl.multiple_of(c * 128, 128), 128)
+    sib_rows = pl.ds(pl.multiple_of((1 - c) * 128, 128), 128)
+
+    def chunk_of(s):
+        near = z + (1 - 2 * z + 4 * half) * s
+        far = 2 - half + (s - 2) * (1 - 2 * half)
+        is_far = lax.div(s, 2)
+        return near * (1 - is_far) + far * is_far
+
+    def remote(src, dst, send, recv, device):
+        return pltpu.make_async_remote_copy(
+            src_ref=src, dst_ref=dst, send_sem=send, recv_sem=recv,
+            device_id=device, device_id_type=MESH,
+        )
+
+    loads = [
+        pltpu.make_async_copy(tokens, x_all.at[z, x, rows], load_sem.at[0]),
+        pltpu.make_async_copy(gate_hbm, gate_w, load_sem.at[1]),
+        pltpu.make_async_copy(up_hbm, up_w, load_sem.at[2]),
+        pltpu.make_async_copy(down_hbm, down_w, load_sem.at[3]),
+        pltpu.make_async_copy(own, wt.at[e], load_sem.at[4]),
+    ]
+    for load in (loads[0], loads[4], loads[1], loads[2], loads[3]):
+        load.start()
+
+    barrier = pltpu.get_barrier_semaphore()
+    for d in range(1, 8):
+        pl.semaphore_signal(
+            barrier, inc=1, device_id={"expert": lax.rem(e + d, 8)}, device_id_type=MESH
+        )
+    pl.semaphore_signal(barrier, inc=1, device_id=x_peer, device_id_type=MESH)
+    pl.semaphore_wait(barrier, 8)
+    loads[0].wait()
+    loads[4].wait()
+
+    def piece(s, h):
+        return x_all.at[chunk_of(s), h, rows]
+
+    def to_right(s):
+        q = chunk_of(s)
+        return remote(piece(s, x), piece(s, x), z_send.at[s, 0], z_recv.at[q],
+                      {"expert": lax.rem(e + 2, 8)})
+
+    def to_left(s):
+        q = chunk_of(s)
+        return remote(piece(s, x), piece(s, x), z_send.at[s, 1], z_recv.at[q],
+                      {"expert": lax.rem(e + 6, 8)})
+
+    def across(s):
+        return remote(piece(s, x), piece(s, x), x_send.at[s], x_recv.at[chunk_of(s)], x_peer)
+
+    def beside(s, k):
+        h = x if k == 0 else other
+        return remote(piece(s, h), piece(s, h), s_send.at[s, k], s_recv.at[chunk_of(s), k], sibling)
+
+    def weight(d):
+        return remote(wt.at[e], wt.at[e], w_send.at[d], w_recv.at[e],
+                      {"expert": lax.rem(e + d, 8)})
+
+    def hidden_copy(s):
+        q = chunk_of(s)
+        return remote(hid.at[q, x], hid.at[q, x], h_send.at[s], h_recv.at[q], x_peer)
+
+    def share_copy(s):
+        return remote(to_sib.at[s], from_sib.at[s], r_send.at[s], r_recv.at[s], sibling)
+
+    def chip_copy(s):
+        return remote(to_chip.at[s], from_chip.at[z], c_send.at[s], c_recv.at[z],
+                      {"expert": chunk_of(s) * 2 + c})
+
+    def goes_right(s):
+        return (chunk_of(s) <= z) & (z < CHIPS - 1)
+
+    def goes_left(s):
+        return (chunk_of(s) >= z) & (z > 0)
+
+    def stage_a(s):
+        q = chunk_of(s)
+
+        @pl.when(s > 0)
+        def _():
+            remote(piece(s, x), piece(s, x), z_send.at[s, 0], z_recv.at[q], x_peer).wait_recv()
+
+        @pl.when(goes_right(s))
+        def _():
+            to_right(s).start()
+
+        @pl.when(goes_left(s))
+        def _():
+            to_left(s).start()
+
+        across(s).start()
+        beside(s, 0).start()
+
+    def stage_b(s):
+        q = chunk_of(s)
+        remote(piece(s, other), piece(s, other), x_send.at[s], x_recv.at[q], x_peer).wait_recv()
+        beside(s, 1).start()
+
+    def stage_c(s):
+        q = chunk_of(s)
+        for k in range(2):
+            h = x if k == 0 else other
+            landed = x_all.at[q, h, sib_rows]
+            remote(landed, landed, s_send.at[s, k], s_recv.at[q, k], sibling).wait_recv()
+
+        @pl.loop(0, gate_w.shape[1] // TILE)
+        def _(i):
+            cols = pl.ds(pl.multiple_of(i * TILE, TILE), TILE)
+            depth = x_all.shape[3]
+            first, second = x_all[q, 0], x_all[q, 1]
+
+            def both(w):
+                return jnp.dot(
+                    first, w[:depth, cols], preferred_element_type=jnp.float32
+                ) + jnp.dot(second, w[depth:, cols], preferred_element_type=jnp.float32)
+
+            g, u = both(gate_w), both(up_w)
+            hid[q, x, :, cols] = (g / (1.0 + jnp.exp(-g)) * u).astype(jnp.bfloat16)
+
+        hidden_copy(s).start()
+
+    def stage_d(s):
+        q = chunk_of(s)
+        slot = lax.rem(s, 2)
+        landed = hid.at[q, other]
+        remote(landed, landed, h_send.at[s], h_recv.at[q], x_peer).wait_recv()
+        eye = lax.broadcasted_iota(jnp.int32, (128, 128), 0) == lax.broadcasted_iota(
+            jnp.int32, (128, 128), 1
+        )
+
+        def column(source):
+            return jnp.sum(jnp.where(eye, wt[source, pl.ds(e, 1), :], 0.0), 1, keepdims=True)
+
+        scale = jnp.concatenate([column(q * 2), column(q * 2 + 1)], 0)
+
+        @pl.loop(0, down_w.shape[1] // DOWN_TILE)
+        def _(i):
+            cols = pl.ds(pl.multiple_of(i * DOWN_TILE, DOWN_TILE), DOWN_TILE)
+            depth = hid.shape[3]
+            part = jnp.dot(
+                hid[q, 0], down_w[:depth, cols], preferred_element_type=jnp.float32
+            ) + jnp.dot(hid[q, 1], down_w[depth:, cols], preferred_element_type=jnp.float32)
+            res[slot, :, cols] = part * scale
+
+        to_sib[s] = res[slot, sib_rows].astype(jnp.bfloat16)
+        share_copy(s).start()
+
+    def stage_e(s):
+        slot = lax.rem(s, 2)
+        share_copy(s).wait_recv()
+        both = res[slot, rows] + from_sib[s].astype(jnp.float32)
+
+        @pl.when(s == 0)
+        def _():
+            acc[...] = both
+
+        @pl.when(s > 0)
+        def _():
+            to_chip[s] = both.astype(jnp.bfloat16)
+            chip_copy(s).start()
+
+    stage_a(jnp.int32(0))
+
+    @pl.loop(1, 8)
+    def _(d):
+        weight(d).start()
+
+    loads[1].wait()
+    loads[2].wait()
+    loads[3].wait()
+
+    @pl.loop(1, 8)
+    def _(d):
+        source = lax.rem(e + d, 8)
+        remote(wt.at[source], wt.at[source], w_send.at[d], w_recv.at[source], sibling).wait_recv()
+
+    @pl.loop(0, CHIPS + 2)
+    def _(t):
+        @pl.when(t < CHIPS - 1)
+        def _():
+            stage_a(t + 1)
+
+        @pl.when(t < CHIPS)
+        def _():
+            stage_b(t)
+            stage_c(t)
+
+        @pl.when((t >= 1) & (t < CHIPS + 1))
+        def _():
+            stage_d(t - 1)
+
+        @pl.when(t >= 2)
+        def _():
+            stage_e(t - 2)
+
+    @pl.loop(1, CHIPS)
+    def _(s):
+        q = chunk_of(s)
+        remote(from_chip.at[q], from_chip.at[q], c_send.at[s], c_recv.at[q], sibling).wait_recv()
+        acc[...] += from_chip[q].astype(jnp.float32)
+
+    out[...] = acc[...].astype(jnp.bfloat16)
+
+    @pl.loop(1, 8)
+    def _(d):
+        weight(d).wait_send()
+
+    @pl.loop(0, CHIPS)
+    def _(s):
+        @pl.when(goes_right(s))
+        def _():
+            to_right(s).wait_send()
+
+        @pl.when(goes_left(s))
+        def _():
+            to_left(s).wait_send()
+
+        across(s).wait_send()
+        beside(s, 0).wait_send()
+        beside(s, 1).wait_send()
+        hidden_copy(s).wait_send()
+        share_copy(s).wait_send()
+
+        @pl.when(s > 0)
+        def _():
+            chip_copy(s).wait_send()
+
+
+def fused(tokens, expert_ids, gates, gate_w, up_w, down_w):
+    rows, feats = tokens.shape
+    hidden, width = gate_w.shape[2], down_w.shape[2]
+    own = jnp.sum(
+        jnp.where(
+            expert_ids.T[None, :, :] == jnp.arange(8, dtype=jnp.int32)[:, None, None],
+            gates.T[None, :, :],
+            0.0,
+        ),
+        1,
+    )
+    dma = pltpu.SemaphoreType.DMA
+    bf16, f32 = jnp.bfloat16, jnp.float32
+    flops = 2 * 8 * rows * (2 * 2 * feats * hidden + 2 * hidden * width)
+    return pl.pallas_call(
+        kernel,
+        out_shape=jax.ShapeDtypeStruct((rows, width), bf16),
+        in_specs=[pl.BlockSpec(memory_space=pl.ANY)] * 5,
+        out_specs=pl.BlockSpec(memory_space=pltpu.VMEM),
+        scratch_shapes=[
+            pltpu.VMEM((CHIPS, 2, 2 * rows, feats), bf16),
+            pltpu.VMEM(gate_w.shape[1:], bf16),
+            pltpu.VMEM(up_w.shape[1:], bf16),
+            pltpu.VMEM(down_w.shape[1:], bf16),
+            pltpu.VMEM((CHIPS, 2, 2 * rows, hidden), bf16),
+            pltpu.VMEM((2, 2 * rows, width), f32),
+            pltpu.VMEM((CHIPS, rows, width), bf16),
+            pltpu.VMEM((CHIPS, rows, width), bf16),
+            pltpu.VMEM((CHIPS, rows, width), bf16),
+            pltpu.VMEM((CHIPS, rows, width), bf16),
+            pltpu.VMEM((rows, width), f32),
+            pltpu.VMEM((8, 8, rows), f32),
+            dma((5,)), dma((4, 2)), dma((4,)), dma((4, 2)), dma((8,)), dma((4,)), dma((4,)), dma((4,)),
+            dma((4,)), dma((4,)), dma((4, 2)), dma((8,)), dma((4,)), dma((4,)), dma((4,)),
+        ],
+        compiler_params=pltpu.CompilerParams(
+            collective_id=0, has_side_effects=True, vmem_limit_bytes=56 * 1024 * 1024
+        ),
+        cost_estimate=pl.CostEstimate(flops=flops, bytes_accessed=20 << 20, transcendentals=1 << 20),
+    )(tokens, own, gate_w[0], up_w[0], down_w[0])
+
+
+def on_device(tokens, expert_ids, gates, gate_w, up_w, down_w):
+    fits = (
+        lax.axis_size("expert") == 8
+        and lax.axis_size("tensor") == 2
+        and tokens.shape == (128, 2048)
+        and gate_w.shape[2] == 768
+    )
+    return (fused if fits else dense)(tokens, expert_ids, gates, gate_w, up_w, down_w)
+
+
 def solution(mesh):
     in_specs = (
         P(("group", "expert"), "tensor"),

time: 250 us -> 144 us (0.58)
  waiting for transfers between devices: 190 us -> 0 us
  Pallas kernels: 0 us -> 140 us
  matrix products: 33 us -> 0 us
  blocking collectives: 14 us -> 0 us
  between operations: 13.2 us -> 0.01 us
    pallas_call x0 -> x1, Pallas kernels: none -> 140 us  [fused(): pl.pallas_call(kernel, out_shape=jax.ShapeDtypeStruct((rows, width), bf16...]
    all_gather x3 -> x0, waiting for transfers between devices: 139 us -> none  [the longest x1 83.6 us: on_device(): rows_all = lax.all_gather(whole, 'expert', axis=0, tiled=True)]
    reduce_scatter x1 -> x0, waiting for transfers between devices: 50.2 us -> none  [on_device(): return lax.psum_scatter(share, 'expert', scatter_dimension=0, tiled=True)]
    dot_general x3 -> x0, matrix products: 33 us -> none  [the longest x1 11 us: on_device(): result = jnp.dot(hidden, down_w[0], preferred_element_type=jnp.float32)]
    all_gather x1 -> x0, blocking collectives: 14 us -> none  [on_device(): lax.all_gather(own, 'expert', axis=0, tiled=True)]
  transfers between devices with their start and end apart: 4 -> 0, of which waited for: 4 -> 0; matrix products, arithmetic and copies ran while one was open for 0% -> 0% of each run, Pallas kernels for 0% -> 0%
where the time goes in v2:
time: 144 us
  Pallas kernels  140 us (97%)
  local copies, waits for them, and re-layouts  1.88 us (1%)
    pallas_call x1, Pallas kernels, fused(): pl.pallas_call(kernel, out_shape=jax.ShapeDtypeStruct((rows, width), bf16...  140 us

profile of v2, /device:TPU:0, one launch (start us, length us, event | category | flops | bytes accessed | tf_op | source)
XLA Modules:
  0.0 143.6 jit_solution(13643555594040263503)
XLA Ops:
  0.0 1.3 select_reduce_fusion.own
  1.3 140.4 %shard_map.64 = bf16[128,2048]{1,0:T(8,128)(2,1)} custom-call(bf16[128,2048]{1,0:T(8,128)(2,1)} %tokens.1, f32[8,128]{1,0:T(8,128)} %select_reduce_fusion.own, bf16[4096,768]{1,0:T(8,128)(2,1)} %bitcast.7, bf16[4096,768]{1,0:T(8,128)(2,1)} %bitcast.8, bf16[1536,2048]{1,0:T(8,128)(2,1)} %bitcast.9), custom_call_target="tpu_custom_call" | custom-call | flops 19327352832 | bytes 20971520 | tf_op jit(solution)/shard_map/pallas_call | solution.py:294
  141.7 1.9 %copy.8 = bf16[128,2048]{1,0:T(8,128)(2,1)} copy(bf16[128,2048]{1,0:T(8,128)(2,1)} %shard_map.64) | data formatting | bytes 1048576

commit v3 on v2

--- a/solution.py
+++ b/solution.py
@@ -33,13 +33,14 @@
 CHIPS = 4
 TILE = 256
 DOWN_TILE = 512
+ALONG = 512
 
 
 def kernel(
     tokens, own, gate_hbm, up_hbm, down_hbm, out,
     x_all, gate_w, up_w, down_w, hid, res, to_sib, from_sib, to_chip, from_chip, acc, wt,
-    load_sem, z_send, x_send, s_send, w_send, h_send, r_send, c_send,
-    z_recv, x_recv, s_recv, w_recv, h_recv, r_recv, c_recv,
+    load_sem, z_send, n_send, x_send, s_send, w_send, h_send, r_send, c_send,
+    z_recv, n_recv, x_recv, s_recv, w_recv, h_recv, r_recv, c_recv,
 ):
     e = lax.axis_index("expert")
     x = lax.axis_index("tensor")
@@ -96,8 +97,20 @@
         return remote(piece(s, x), piece(s, x), z_send.at[s, 1], z_recv.at[q],
                       {"expert": lax.rem(e + 6, 8)})
 
-    def across(s):
-        return remote(piece(s, x), piece(s, x), x_send.at[s], x_recv.at[chunk_of(s)], x_peer)
+    def along(s):
+        return x_all.at[chunk_of(s), other, rows, pl.ds(0, ALONG)]
+
+    def along_to(s, side):
+        return remote(along(s), along(s), n_send.at[s, side], n_recv.at[chunk_of(s)],
+                      {"expert": lax.rem(e + (2 if side == 0 else 6), 8)})
+
+    def across_own():
+        return remote(piece(0, x), piece(0, x), x_send.at[0], x_recv.at[z], x_peer)
+
+    def across(s, h):
+        q = chunk_of(s)
+        part = x_all.at[q, h, rows, pl.ds(ALONG, x_all.shape[3] - ALONG)]
+        return remote(part, part, x_send.at[s], x_recv.at[q], x_peer)
 
     def beside(s, k):
         h = x if k == 0 else other
@@ -139,12 +152,38 @@
         def _():
             to_left(s).start()
 
-        across(s).start()
+        @pl.when(s == 0)
+        def _():
+            across_own().start()
+
+        @pl.when(s > 0)
+        def _():
+            across(s, x).start()
+
         beside(s, 0).start()
 
     def stage_b(s):
-        q = chunk_of(s)
-        remote(piece(s, other), piece(s, other), x_send.at[s], x_recv.at[q], x_peer).wait_recv()
+        @pl.when(s == 0)
+        def _():
+            mine = piece(0, other)
+            remote(mine, mine, x_send.at[0], x_recv.at[z], x_peer).wait_recv()
+
+        @pl.when(s > 0)
+        def _():
+            remote(along(s), along(s), n_send.at[s, 0], n_recv.at[chunk_of(s)], x_peer).wait_recv()
+
+        @pl.when(goes_right(s))
+        def _():
+            along_to(s, 0).start()
+
+        @pl.when(goes_left(s))
+        def _():
+            along_to(s, 1).start()
+
+        @pl.when(s > 0)
+        def _():
+            across(s, other).wait_recv()
+
         beside(s, 1).start()
 
     def stage_c(s):
@@ -168,11 +207,8 @@
             g, u = both(gate_w), both(up_w)
             hid[q, x, :, cols] = (g / (1.0 + jnp.exp(-g)) * u).astype(jnp.bfloat16)
 
-        hidden_copy(s).start()
-
-    def stage_d(s):
-        q = chunk_of(s)
-        slot = lax.rem(s, 2)
+    def stage_d(s, slot):
+        q = chunk_of(s)
         landed = hid.at[q, other]
         remote(landed, landed, h_send.at[s], h_recv.at[q], x_peer).wait_recv()
         eye = lax.broadcasted_iota(jnp.int32, (128, 128), 0) == lax.broadcasted_iota(
@@ -196,8 +232,7 @@
         to_sib[s] = res[slot, sib_rows].astype(jnp.bfloat16)
         share_copy(s).start()
 
-    def stage_e(s):
-        slot = lax.rem(s, 2)
+    def stage_e(s, slot):
         share_copy(s).wait_recv()
         both = res[slot, rows] + from_sib[s].astype(jnp.float32)
 
@@ -225,24 +260,37 @@
         source = lax.rem(e + d, 8)
         remote(wt.at[source], wt.at[source], w_send.at[d], w_recv.at[source], sibling).wait_recv()
 
-    @pl.loop(0, CHIPS + 2)
+    @pl.loop(0, CHIPS)
     def _(t):
         @pl.when(t < CHIPS - 1)
         def _():
             stage_a(t + 1)
 
-        @pl.when(t < CHIPS)
-        def _():
-            stage_b(t)
-            stage_c(t)
-
-        @pl.when((t >= 1) & (t < CHIPS + 1))
-        def _():
-            stage_d(t - 1)
+        stage_b(t)
+        stage_c(t)
 
         @pl.when(t >= 2)
         def _():
-            stage_e(t - 2)
+            hidden_copy(t).start()
+
+        @pl.when(t == CHIPS - 1)
+        def _():
+            hidden_copy(jnp.int32(1)).start()
+            hidden_copy(jnp.int32(0)).start()
+
+    def turn(u):
+        late = lax.div(u, 2)
+        return (u + 2) * (1 - late) + (3 - u) * late
+
+    @pl.loop(0, CHIPS + 1)
+    def _(u):
+        @pl.when(u < CHIPS)
+        def _():
+            stage_d(turn(u), lax.rem(u, 2))
+
+        @pl.when(u > 0)
+        def _():
+            stage_e(turn(u - 1), lax.rem(u - 1, 2))
 
     @pl.loop(1, CHIPS)
     def _(s):
@@ -261,12 +309,21 @@
         @pl.when(goes_right(s))
         def _():
             to_right(s).wait_send()
+            along_to(s, 0).wait_send()
 
         @pl.when(goes_left(s))
         def _():
             to_left(s).wait_send()
-
-        across(s).wait_send()
+            along_to(s, 1).wait_send()
+
+        @pl.when(s == 0)
+        def _():
+            across_own().wait_send()
+
+        @pl.when(s > 0)
+        def _():
+            across(s, x).wait_send()
+
         beside(s, 0).wait_send()
         beside(s, 1).wait_send()
         hidden_copy(s).wait_send()
@@ -309,8 +366,8 @@
             pltpu.VMEM((CHIPS, rows, width), bf16),
             pltpu.VMEM((rows, width), f32),
             pltpu.VMEM((8, 8, rows), f32),
-            dma((5,)), dma((4, 2)), dma((4,)), dma((4, 2)), dma((8,)), dma((4,)), dma((4,)), dma((4,)),
-            dma((4,)), dma((4,)), dma((4, 2)), dma((8,)), dma((4,)), dma((4,)), dma((4,)),
+            dma((5,)), dma((4, 2)), dma((4, 2)), dma((4,)), dma((4, 2)), dma((8,)), dma((4,)), dma((4,)), dma((4,)),
+            dma((4,)), dma((4,)), dma((4,)), dma((4, 2)), dma((8,)), dma((4,)), dma((4,)), dma((4,)),
         ],
         compiler_params=pltpu.CompilerParams(
             collective_id=0, has_side_effects=True, vmem_limit_bytes=56 * 1024 * 1024

time: 144 us -> 120 us (0.83)
  Pallas kernels: 140 us -> 116 us
    pallas_call x1, Pallas kernels: 140 us -> 116 us  [fused(): pl.pallas_call(kernel, out_shape=jax.ShapeDtypeStruct((rows, width), bf16...]
where the time goes in v3:
time: 120 us; the launch traced here: 119 us
  Pallas kernels  116 us (97%)
  local copies, waits for them, and re-layouts  1.88 us (2%)
  other arithmetic  1.3 us (1%)
    pallas_call x1, Pallas kernels, fused(): pl.pallas_call(kernel, out_shape=jax.ShapeDtypeStruct((rows, width), bf16...  116 us

profile of v3, /device:TPU:0, one launch (start us, length us, event | category | flops | bytes accessed | tf_op | source)
XLA Modules:
  0.0 119.4 jit_solution(2742867852553043587)
XLA Ops:
  0.0 1.3 %select_reduce_fusion.own = f32[8,128]{1,0:T(8,128)} fusion(f32[4,128]{1,0:T(4,128)} %bitcast.5, s32[4,128]{1,0:T(4,128)} %bitcast.6), kind=kLoop, calls=%fused_computation | loop fusion | flops 11264 | bytes 8192 | tf_op jit(solution)/shard_map/reduce_sum | solution.py:340
  1.3 116.2 %shard_map.64 = bf16[128,2048]{1,0:T(8,128)(2,1)} custom-call(bf16[128,2048]{1,0:T(8,128)(2,1)} %tokens.1, f32[8,128]{1,0:T(8,128)} %select_reduce_fusion.own, bf16[4096,768]{1,0:T(8,128)(2,1)} %bitcast.7, bf16[4096,768]{1,0:T(8,128)(2,1)} %bitcast.8, bf16[1536,2048]{1,0:T(8,128)(2,1)} %bitcast.9), custom_call_target="tpu_custom_call" | custom-call | flops 19327352832 | bytes 20971520 | tf_op jit(solution)/shard_map/pallas_call | solution.py:351
  117.5 1.9 %copy.8 = bf16[128,2048]{1,0:T(8,128)(2,1)} copy(bf16[128,2048]{1,0:T(8,128)(2,1)} %shard_map.64) | data formatting | bytes 1048576

commit v4 on v3

--- a/solution.py
+++ b/solution.py
@@ -282,15 +282,10 @@
         late = lax.div(u, 2)
         return (u + 2) * (1 - late) + (3 - u) * late
 
-    @pl.loop(0, CHIPS + 1)
+    @pl.loop(0, CHIPS)
     def _(u):
-        @pl.when(u < CHIPS)
-        def _():
-            stage_d(turn(u), lax.rem(u, 2))
-
-        @pl.when(u > 0)
-        def _():
-            stage_e(turn(u - 1), lax.rem(u - 1, 2))
+        stage_d(turn(u), lax.rem(u, 2))
+        stage_e(turn(u), lax.rem(u, 2))
 
     @pl.loop(1, CHIPS)
     def _(s):

time: 120 us -> 113 us (0.942)
  Pallas kernels: 116 us -> 110 us
    pallas_call x1, Pallas kernels: 116 us -> 110 us  [fused(): pl.pallas_call(kernel, out_shape=jax.ShapeDtypeStruct((rows, width), bf16...]
where the time goes in v4:
time: 113 us
  Pallas kernels  110 us (97%)
  local copies, waits for them, and re-layouts  1.88 us (2%)
  other arithmetic  1.3 us (1%)
    pallas_call x1, Pallas kernels, fused(): pl.pallas_call(kernel, out_shape=jax.ShapeDtypeStruct((rows, width), bf16...  110 us

profile of v4, /device:TPU:0, one launch (start us, length us, event | category | flops | bytes accessed | tf_op | source)
XLA Modules:
  0.0 112.8 jit_solution(15444233197288295784)
XLA Ops:
  0.0 1.3 %select_reduce_fusion.own = f32[8,128]{1,0:T(8,128)} fusion(f32[4,128]{1,0:T(4,128)} %bitcast.5, s32[4,128]{1,0:T(4,128)} %bitcast.6), kind=kLoop, calls=%fused_computation | loop fusion | flops 11264 | bytes 8192 | tf_op jit(solution)/shard_map/reduce_sum | solution.py:335
  1.3 109.6 %shard_map.64 = bf16[128,2048]{1,0:T(8,128)(2,1)} custom-call(bf16[128,2048]{1,0:T(8,128)(2,1)} %tokens.1, f32[8,128]{1,0:T(8,128)} %select_reduce_fusion.own, bf16[4096,768]{1,0:T(8,128)(2,1)} %bitcast.7, bf16[4096,768]{1,0:T(8,128)(2,1)} %bitcast.8, bf16[1536,2048]{1,0:T(8,128)(2,1)} %bitcast.9), custom_call_target="tpu_custom_call" | custom-call | flops 19327352832 | bytes 20971520 | tf_op jit(solution)/shard_map/pallas_call | solution.py:346
  110.9 1.9 %copy.8 = bf16[128,2048]{1,0:T(8,128)(2,1)} copy(bf16[128,2048]{1,0:T(8,128)(2,1)} %shard_map.64) | data formatting | bytes 1048576
